TPU v7x, 256 devices: a whole 4x4x8 slice. The times are simulated.
256 devices in a mesh: member: 64 (over x, z_hi, y), lon: 4 (over z_lo, core).
Axes of the slice: x: 4, y: 4, z: 8 (z_hi: 4, z_lo: 2; z = z_hi * 2 + z_lo), core: 2. Of those that a mesh axis runs over, the one named last changes fastest.
Arguments:
- air_temp: bfloat16 [64, 4, 64, 2048], P('member', None, None, 'lon'), may hold values from -6 to 6
- air_humid: bfloat16 [64, 4, 64, 2048], P('member', None, None, 'lon'), may hold values from -6 to 6
- wind: bfloat16 [64, 2, 64, 2048], P('member', None, None, 'lon'), may hold values from -6 to 6
- exchange_coef: float32 [64], P('member'), may hold values from 0.5 to 2
- sea_surface_anomaly: float32 [64, 2048], P('member', 'lon'), may hold values from -6 to 6
- sea_ice: float32 [64, 2048], P('member', 'lon'), may hold values from 0 to 1
- current: float32 [2, 64, 2048], P(None, 'member', 'lon'), may hold values from -3 to 3
- surface_mask: int32 [64, 2048], P(None, 'lon'), may hold values from 0 to 2
Outputs:
- deepest_layer_warmth: float32 [64, 64, 2048], P('member', None, 'lon')
- bottom_level_humidity: float32 [64, 64, 2048], P('member', None, 'lon')
- averaged_flux_vector: float32 [4, 64, 2048], P(None, 'member', 'lon')
- sea_surface_temp_updated: float32 [64, 2048], P('member', 'lon')
All inputs are finite; a program needn't handle non-finite values.
Results may differ from a plain program's by a relative error of at most 0.0003.
Values sent between devices are 32-bit elements; how exact they have to be, the bound alone decides.
A program may use at most 64 MiB of HBM per device.

v0:
```python
import jax
import jax.numpy as jnp
from jax import lax
from jax.sharding import PartitionSpec as P

LEV = 4
STEPS = 2


diffusion_coef = 0.2
half_courant = 0.1
interval_length = 0.1
vertical_mix = 1.0
advance_ocean_column = 0.5
saturation = 0.5


def with_halo(cells, sides, width):
    for axis, dim in sides:
        count = lax.axis_size(axis)
        head = lax.slice_in_dim(cells, 0, width, axis=dim)
        tail = lax.slice_in_dim(cells, cells.shape[dim] - width, cells.shape[dim], axis=dim)
        cells = jnp.concatenate(
            [
                lax.ppermute(tail, axis, [(i, (i + 1) % count) for i in range(count)]),
                cells,
                lax.ppermute(head, axis, [((i + 1) % count, i) for i in range(count)]),
            ],
            axis=dim,
        )
    return cells


def vertical(state):
    levels = [state[:, k] for k in range(LEV)]
    diags = [1.0 + 2.0 * vertical_mix for k in range(LEV)]
    diags[0] = 1.0 + vertical_mix
    diags[LEV - 1] = 1.0 + vertical_mix
    cprime = []
    modified_right_hand = []
    for k in range(LEV):
        if k == 0:
            denom = diags[0]
            modified_right_hand.append(levels[0] / denom)
        else:
            denom = diags[k] + vertical_mix * cprime[k - 1]
            modified_right_hand.append(
                (levels[k] + vertical_mix * modified_right_hand[k - 1]) / denom
            )
        cprime.append(-vertical_mix / denom)
    result = [None] * LEV
    result[LEV - 1] = modified_right_hand[LEV - 1]
    for k in range(LEV - 2, -1, -1):
        result[k] = modified_right_hand[k] - cprime[k] * result[k + 1]
    return jnp.stack(result, axis=1)


def advect_core(state, east, west, u_wind, v_wind):
    north = jnp.concatenate([state[..., 1:, :], state[..., -1:, :]], axis=-2)
    south = jnp.concatenate([state[..., :1, :], state[..., :-1, :]], axis=-2)
    lapl = east + west + north + south - 4.0 * state
    return (
        state
        + diffusion_coef * lapl
        - half_courant * (u_wind * (east - west) + v_wind * (north - south))
    )


def advect(state, u_wind, v_wind):
    padded = with_halo(state, (("lon", 3),), 1)
    return advect_core(state, padded[..., 2:], padded[..., :-2], u_wind, v_wind)


def on_device(
    air_temp, air_humid, wind, exchange_coef, sea_surface_anomaly, sea_ice, current, surface_mask
):
    local_members = air_temp.shape[0]
    own_rows = sea_surface_anomaly.shape[0]
    full_temp, full_ice, full_current = (
        lax.all_gather(sea_surface_anomaly, "member", axis=0, tiled=True),
        lax.all_gather(sea_ice, "member", axis=0, tiled=True),
        lax.all_gather(current, "member", axis=1, tiled=True),
    )
    seafrac = (surface_mask == 1).astype(jnp.float32) + (surface_mask == 2).astype(jnp.float32) * (
        1.0 - full_ice
    )
    member_idx = 0
    state = jnp.stack([air_temp[member_idx], air_humid[member_idx]]).astype(jnp.float32)
    u_wind = wind[member_idx, 0].astype(jnp.float32)
    v_wind = wind[member_idx, 1].astype(jnp.float32)
    winds = [(u_wind, v_wind)]
    rel_u = u_wind - full_current[0]
    rel_v = v_wind - full_current[1]
    speed = jnp.sqrt(rel_u * rel_u + rel_v * rel_v + 1.0)
    drag = exchange_coef[member_idx] * speed * seafrac
    drags = [drag]
    stresses = [(drag * rel_u, drag * rel_v)]
    model_conditions = [state]
    total = jnp.zeros((4,) + seafrac.shape, jnp.float32)
    for step in range(STEPS):
        member_idx = 0
        state = advect(model_conditions[member_idx], winds[member_idx][0], winds[member_idx][1])
        drag = drags[member_idx]
        heat = drag * (full_temp - state[0, 0])
        fresh = drag * (saturation * full_temp - state[1, 0])
        state = state.at[0, 0].add(interval_length * heat)
        state = state.at[1, 0].add(interval_length * fresh)
        model_conditions[member_idx] = vertical(state)
        step_flux = jnp.stack([heat, fresh, stresses[member_idx][0], stresses[member_idx][1]])
        total = total + step_flux
    summed = lax.psum(total, "member")
    owned = lax.dynamic_slice_in_dim(summed, lax.axis_index("member") * own_rows, own_rows, 1)
    count = local_members * lax.axis_size("member") * STEPS
    averaged_flux_vector = owned / jnp.float32(count)
    sea_surface_temp_updated = sea_surface_anomaly - advance_ocean_column * averaged_flux_vector[0]
    deepest_layer_warmth = jnp.stack([surface_entry[0, 0] for surface_entry in model_conditions])
    bottom_level_humidity = jnp.stack([surface_entry[1, 0] for surface_entry in model_conditions])
    return (
        deepest_layer_warmth,
        bottom_level_humidity,
        averaged_flux_vector,
        sea_surface_temp_updated,
    )


def solution(mesh):
    in_specs = (
        P("member", None, None, "lon"),
        P("member", None, None, "lon"),
        P("member", None, None, "lon"),
        P("member"),
        P("member", "lon"),
        P("member", "lon"),
        P(None, "member", "lon"),
        P(None, "lon"),
    )
    out_specs = (
        P("member", None, "lon"),
        P("member", None, "lon"),
        P(None, "member", "lon"),
        P("member", "lon"),
    )
    return jax.shard_map(
        on_device, mesh=mesh, in_specs=in_specs, out_specs=out_specs, check_vma=False
    )
```

profile of v0, /device:TPU:8, one launch (start us, length us, event | category | flops | bytes accessed | tf_op | source)
XLA Modules:
  0.0 1329.2 jit_solution(16603193992028732626)
XLA Ops:
  7.2 0.0 all-reduce.2.cloned.1.call-start
  7.2 1.1 maximum_convert_fusion
  8.3 0.9 fusion.40
  9.2 1.4 collective-permute-start
  10.6 0.0 collective-permute-start.1
  10.6 0.0 copy-start
  10.6 0.2 fusion.41
  10.8 0.6 fusion.42
  11.4 0.0 copy-done
  11.5 0.0 copy-start.7
  11.5 0.7 copy-done.7
  12.1 0.0 copy-start.9
  12.1 189.7 %all-gather.1 = f32[64,1,512]{2,1,0:T(1,128)S(1)} all-gather(f32[1,1,512]{2,1,0:T(1,128)S(1)} %bitcast.197), channel_id=1, replica_groups=mesh['member'=64,'lon'=4] {'member'}, dimensions={0}, use_global_device_ids=true | all-gather | bytes 133120 | tf_op jit(solution)/shard_map/all_gather | solution.py:80
  201.8 0.0 copy-done.9
  201.8 190.2 %all_gather.9 = f32[2,64,512]{2,0,1:T(2,128)S(1)} all-gather(f32[2,1,512]{2,0,1:T(2,128)S(1)} %copy.34), channel_id=1, replica_groups=mesh['member'=64,'lon'=4] {'member'}, dimensions={1}, use_global_device_ids=true | all-gather | bytes 266240 | tf_op jit(solution)/shard_map/all_gather | solution.py:82
  392.0 0.0 copy-start.10
  392.0 0.9 fusion.44
  392.9 0.0 copy-done.10
  392.9 194.2 %all-gather = f32[64,1,512]{2,1,0:T(1,128)} all-gather(f32[1,1,512]{2,1,0:T(1,128)S(1)} %bitcast.198), channel_id=1, replica_groups=mesh['member'=64,'lon'=4] {'member'}, dimensions={0}, use_global_device_ids=true | all-gather | bytes 133120 | tf_op jit(solution)/shard_map/all_gather | solution.py:81
  587.8 0.0 collective-permute-done
  587.8 0.0 collective-permute-done.1
  587.8 1.9 multiply_subtract_fusion
  589.7 0.0 copy-start.1
  589.7 0.0 copy-start.2
  589.8 0.0 copy-start.3
  589.8 0.0 copy-start.4
  589.8 0.0 copy-start.5
  589.8 0.1 copy.107
  589.9 0.8 copy-done.1
  590.6 0.1 copy-done.2
  590.7 0.1 copy-done.3
  590.8 0.1 copy-done.4
  590.8 0.1 copy-done.5
  590.9 0.1 fusion.33
  591.1 0.1 fusion.22
  591.2 0.1 bitcast_subtract_fusion
  591.4 0.1 fusion.30
  591.4 0.1 fusion.37
  591.6 0.2 fusion.38
  591.8 0.1 pad_maximum_fusion.6
  591.9 0.1 collective-permute-start.2
  592.0 0.5 collective-permute-start.3
  592.6 0.1 copy.44
  592.7 5.7 collective-permute-done.2
  598.4 1.7 collective-permute-done.3
  600.1 0.9 subtract_multiply_fusion
  601.0 0.4 copy_subtract_fusion
  601.4 0.1 fusion.34
  601.5 0.1 copy.55
  601.5 0.9 fusion
  602.4 0.0 all-reduce.2.cloned.1.call-update
  602.5 0.1 fusion.19
  602.6 0.1 fusion.7
  602.7 0.7 fusion.43
  603.4 0.0 copy-start.8
  603.4 717.5 %all-reduce.2.cloned.1.call-done = f32[4,64,512]{2,1,0:T(8,128)} async-done(((f32[4,64,512]{2,1,0:T(8,128)}), f32[4,64,512]{2,1,0:T(8,128)}) %all-reduce.2.cloned.1.call-update) | async-done | bytes 524304 | tf_op jit(solution)/shard_map/psum | solution.py:111
  1320.9 0.8 dynamic-slice_multiply_fusion
  1321.8 0.0 copy-done.8
  1321.8 0.0 copy-start.6
  1321.8 0.6 fusion.32
  1322.4 0.0 copy-done.6
  (6 shorter events, 0.1 us)
Async XLA Ops:
  7.2 1313.8 %all-reduce.2.cloned.1.call-start = ((), (), s32[]{:S(2)}) async-start(), calls=%async_computation | async-start | bytes 1048576 | tf_op jit(solution)/shard_map/psum | solution.py:111
  9.2 578.6 %collective-permute-start = (f32[2,4,64,1]{3,2,1,0:T(8,128)}, f32[2,4,64,1]{3,2,1,0:T(8,128)}, u32[]{:S(2)}, u32[]{:S(2)}) collective-permute-start(f32[2,4,64,1]{3,2,1,0:T(8,128)} %get-tuple-element.68), channel_id=1, source_target_pairs={{1,0},{2,1},{3,2},{0,3},{5,4},{6,5},{7,6},{4,7},{9,8},{10,9},{11,1... | collective-permute-start | bytes 6152 | tf_op jit(solution)/shard_map/ppermute | solution.py:27
  10.6 577.2 %collective-permute-start.1 = (f32[2,4,64,1]{3,2,1,0:T(8,128)}, f32[2,4,64,1]{3,2,1,0:T(8,128)}, u32[]{:S(2)}, u32[]{:S(2)}) collective-permute-start(f32[2,4,64,1]{3,2,1,0:T(8,128)} %get-tuple-element.67), channel_id=1, source_target_pairs={{0,1},{1,2},{2,3},{3,0},{4,5},{5,6},{6,7},{7,4},{8,9},{9,10},{10,1... | collective-permute-start | bytes 6152 | tf_op jit(solution)/shard_map/ppermute | solution.py:25
  10.6 0.9 copy-start
  11.5 0.7 copy-start.7
  12.1 189.7 %copy-start.9 = (f32[2,1,512]{2,1,0:T(1,128)S(1)}, f32[2,1,512]{2,1,0:T(1,128)}, u32[]{:S(2)}) copy-start(f32[2,1,512]{2,1,0:T(1,128)} %param.22) | copy-start | bytes 12292
  392.0 0.9 copy-start.10
  589.7 0.9 copy-start.1
  589.7 1.0 copy-start.2
  589.8 1.0 copy-start.3
  589.8 1.1 copy-start.4
  589.8 1.1 copy-start.5
  591.9 6.4 collective-permute-start.2
  592.0 8.1 collective-permute-start.3
  603.4 718.4 %copy-start.8 = (f32[1,512]{1,0:T(1,128)S(1)}, f32[1,512]{1,0:T(1,128)}, u32[]{:S(2)}) copy-start(f32[1,512]{1,0:T(1,128)} %param.20) | copy-start | bytes 6148
  1321.8 0.6 copy-start.6
Sparse Core Ops, SparseCore 0:
  602.6 718.3 all-reduce.1
where the time goes:
time: 1330 us
  waiting for transfers between devices  725 us (55%)
  blocking collectives  574 us (43%)
  between operations  14.9 us (1%)
    psum x1, waiting for transfers between devices, on_device(): summed = lax.psum(total, 'member')  718 us
    all_gather x1, blocking collectives, on_device(): lax.all_gather(sea_ice, 'member', axis=0, tiled=True)  194 us
    all_gather x1, blocking collectives, on_device(): lax.all_gather(current, 'member', axis=1, tiled=True)  190 us
    all_gather x1, blocking collectives, on_device(): lax.all_gather(sea_surface_anomaly, 'member', axis=0, tiled=True)  190 us
  transfers between devices with their start and end apart: 5, of which 3 were waited for; matrix products, arithmetic and copies ran while one was open for 0% of the time, Pallas kernels for 0%

commit v1 on v0

v1 whole, which is shorter than its diff:
```python
import jax
import jax.numpy as jnp
from jax import lax
from jax.experimental import pallas as pl
from jax.experimental.pallas import tpu as pltpu
from jax.sharding import PartitionSpec as P

MESH = pl.DeviceIdType.MESH

LAT = 64
LEV = 4
SLAB = 512
MEMBERS = 64
STEPS = 2

SOLVE = (13.0, 5.0, 2.0, 1.0)
SOLVE_TWICE = (199.0, 125.0, 71.0, 46.0)
C00 = 0.1 * 13.0 / 21.0
D00 = 0.1 * 199.0 / 441.0

ROWS = (LAT + 2) * 8
XY = [(a, b) for a in (2, 1, 3, 0) for b in (2, 1, 3, 0) if a or b]


def kernel(
    temp_hbm, humid_hbm, wind_hbm, coef_ref, sst_hbm, ice_hbm, cur_hbm, mask_hbm,
    out_temp_hbm, out_humid_hbm, flux_ref, sst_new_ref,
    temp, humid, wind, mask, own_cur, own_sst, own_ice,
    x0, xp, xq, bp, bq, a1, a2p, a2q, h1, drag, gap, final, uv, ce, cn, m1, m2,
    gathered, stress, heat, got, part, got_z, edge, edge_in, out_temp, out_humid,
    in_sem, out_sem, z_send, z_recv, xy_send, xy_recv, lon_send, lon_recv, red_send, red_recv, redz_send, redz_recv,
):
    m = lax.axis_index("member")
    lon = lax.axis_index("lon")
    x, z, y = m // 16, (m // 4) % 4, m % 4

    def z_peer(d):
        return (x * 16 + ((z + d) % 4) * 4 + y, lon)

    def xy_peer(a, b):
        return (((x + a) % 4) * 16 + z * 4 + (y + b) % 4, lon)

    def lon_peer(d):
        return (m, (lon + d) % 4)

    loads = [
        pltpu.make_async_copy(src, dst, in_sem.at[i])
        for i, (src, dst) in enumerate(
            [
                (cur_hbm, own_cur),
                (sst_hbm, own_sst),
                (ice_hbm, own_ice),
                (wind_hbm, wind),
                (temp_hbm, temp),
                (humid_hbm, humid),
                (mask_hbm, mask),
            ]
        )
    ]
    for copy in loads:
        copy.start()

    barrier = pltpu.get_barrier_semaphore()
    peers = (
        [z_peer(d) for d in (2, 1, 3)]
        + [xy_peer(a, b) for a, b in XY]
        + [lon_peer(d) for d in (1, 3)]
    )
    for peer in peers:
        pl.semaphore_signal(barrier, inc=1, device_id=peer, device_id_type=MESH)

    def remote(src, dst, send, recv, peer):
        return pltpu.make_async_remote_copy(
            src_ref=src, dst_ref=dst, send_sem=send, recv_sem=recv, device_id=peer, device_id_type=MESH
        )

    sub = lax.broadcasted_iota(jnp.int32, (8, 128), 0)
    lane = lax.broadcasted_iota(jnp.int32, (8, 128), 1)
    first_run = (sub % 4) == 0
    last_run = (sub % 4) == 3
    upper = sub < 4
    lane_first = lane == 0
    lane_last = lane == 127
    slot_of = jnp.where(first_run, lane, jnp.where(last_run, (lane + 1) % 128, -1))

    def spread(ref, start, value):
        for c in range(4):
            ref[pl.ds(start + c, 8, stride=8), :] = value[:, c * 128 : (c + 1) * 128]

    def rows_of(ref, j0, shift=1):
        return ref[pl.ds(pl.multiple_of((j0 + shift) * 8, 8), 64), :].reshape(8, 8, 128)

    def put(ref, j0, value):
        ref[pl.ds(pl.multiple_of((j0 + 1) * 8, 8), 64), :] = value.reshape(64, 128)

    def close(ref):
        ref[0:8, :] = ref[8:16, :]
        ref[ROWS - 8 : ROWS, :] = ref[ROWS - 16 : ROWS - 8, :]

    def pack(packed, j0, tiles):
        for k in range(8):
            packed = jnp.where(slot_of == j0 + k, pltpu.roll(tiles[k], j0 + k, 1), packed)
        return packed

    def merge(i):
        from_west = pltpu.roll(pltpu.roll(edge_in[0, i], 5, 0), 1, 1)
        from_east = pltpu.roll(pltpu.roll(edge_in[1, i], 3, 0), 127, 1)
        return jnp.where(first_run, from_west, from_east)

    def advect(ref, j0, halo):
        centre, north, south = rows_of(ref, j0), rows_of(ref, j0, 2), rows_of(ref, j0, 0)
        eastward, northward = rows_of(ce, j0), rows_of(cn, j0)
        result = []
        for k in range(8):
            c = centre[k]
            own_halo = pltpu.roll(halo, (128 - (j0 + k)) % 128, 1)
            right = pltpu.roll(c, 1, 1)
            left = pltpu.roll(c, 127, 1)
            west = jnp.where(lane_first, jnp.where(first_run, own_halo, pltpu.roll(right, 1, 0)), right)
            east = jnp.where(lane_last, jnp.where(last_run, own_halo, pltpu.roll(left, 7, 0)), left)
            result.append(
                0.2 * c
                + 0.4 * (west + south[k])
                + eastward[k] * (east - west)
                + northward[k] * (north[k] - south[k])
            )
        return jnp.stack(result)

    for copy in loads[3:6]:
        copy.wait()

    def prepare(i, carry):
        r0 = pl.multiple_of(i * 16, 16)
        for f, source in ((0, temp), (1, humid)):
            levels = [source[0, k, pl.ds(r0, 16), :].astype(jnp.float32) for k in range(LEV)]
            once = sum(SOLVE[k] * levels[k] for k in range(LEV)) * (1.0 / 21.0)
            twice = sum(SOLVE_TWICE[k] * levels[k] for k in range(LEV)) * (1.0 / 441.0)
            for h in range(2):
                start = (r0 + 8 * h + 1) * 8 + 4 * f
                for ref, value in ((x0, levels[0]), (xp, once), (xq, twice)):
                    spread(ref, start, value[8 * h : 8 * h + 8])
        u = wind[0, 0, pl.ds(r0, 16), :].astype(jnp.float32)
        v = wind[0, 1, pl.ds(r0, 16), :].astype(jnp.float32)
        for h in range(2):
            start = (r0 + 8 * h + 1) * 8
            own = slice(8 * h, 8 * h + 8)
            spread(uv, start, u[own])
            spread(uv, start + 4, v[own])
            for f in range(2):
                spread(ce, start + 4 * f, 0.2 - 0.1 * u[own])
                spread(cn, start + 4 * f, 0.2 - 0.1 * v[own])
        return carry

    lax.fori_loop(0, LAT // 16, prepare, 0)
    for ref in (x0, xp, xq):
        close(ref)

    def pack_inputs(i, packed):
        j0 = i * 8
        return tuple(pack(t, j0, rows_of(ref, j0)) for t, ref in zip(packed, (x0, xp, xq)))

    zero = jnp.zeros((8, 128), jnp.float32)
    packed = lax.fori_loop(0, LAT // 8, pack_inputs, (zero, zero, zero))
    for i in range(3):
        edge[i] = packed[i]

    for copy in loads[:3]:
        copy.wait()
    gathered[x, z, y, 0:8, :] = own_cur[...]
    gathered[x, z, y, 8:12, :] = own_sst[...]
    gathered[x, z, y, 12:16, :] = own_ice[...]

    pl.semaphore_wait(barrier, len(peers))

    sends = []

    def begin(copy):
        copy.start()
        sends.append(copy)
        return copy

    def forward(i, row_z):
        row = gathered.at[x, row_z, y]
        return [
            begin(remote(row, row, xy_send.at[i, n], xy_recv.at[i, n], xy_peer(a, b)))
            for n, (a, b) in enumerate(XY)
        ]

    def exchange(first, count, turn):
        return [
            begin(
                remote(
                    edge.at[pl.ds(first, count)],
                    edge_in.at[s, pl.ds(first, count)],
                    lon_send.at[turn, s],
                    lon_recv.at[turn, s],
                    lon_peer(d),
                )
            )
            for s, d in ((0, 1), (1, 3))
        ]

    own_row = gathered.at[x, z, y]
    along_z = {
        d: begin(remote(own_row, own_row, z_send.at[d - 1], z_recv.at[d - 1], z_peer(d))) for d in (2, 1, 3)
    }
    halos = exchange(0, 3, 0)
    gathers = forward(0, z)

    loads[6].wait()

    def masks(i, carry):
        r0 = pl.multiple_of(i * 8, 8)
        kind = mask[pl.ds(r0, 8), :]
        start = (r0 + 1) * 8
        sea = jnp.where((kind == 1) | (kind == 2), 1.0, 0.0)
        icy = jnp.where(kind == 2, 1.0, 0.0)
        for f in range(2):
            spread(m1, start + 4 * f, sea)
            spread(m2, start + 4 * f, icy)
        return carry

    lax.fori_loop(0, LAT // 8, masks, 0)

    for copy in halos:
        copy.wait_recv()
    halo = [merge(i) for i in range(3)]

    def first_step(i, packed):
        j0 = i * 8
        put(a1, j0, advect(x0, j0, halo[0]))
        moved_p = advect(xp, j0, halo[1])
        put(bp, j0, moved_p)
        moved_q = advect(xq, j0, halo[2])
        put(bq, j0, moved_q)
        return pack(packed[0], j0, moved_p), pack(packed[1], j0, moved_q)

    packed = lax.fori_loop(0, LAT // 8, first_step, (zero, zero))
    for i in range(2):
        edge[3 + i] = packed[i]
    halos = exchange(3, 2, 1)
    close(bp)
    close(bq)

    for i, d in ((1, 1), (2, 3), (3, 2)):
        along_z[d].wait_recv()
        gathers += forward(i, (z - d + 4) % 4)

    for copy in halos:
        copy.wait_recv()
    halo = [merge(3), merge(4)]

    def second_step(i, carry):
        j0 = i * 8
        put(a2p, j0, advect(bp, j0, halo[0]))
        put(a2q, j0, advect(bq, j0, halo[1]))
        return carry

    lax.fori_loop(0, LAT // 8, second_step, 0)

    for copy in gathers:
        copy.wait_recv()

    coef = coef_ref[0]

    def fluxes(i, packed):
        j0 = i * 8
        ix, iz = i // 2, (i % 2) * 2
        block = gathered[ix, pl.ds(iz, 2)].reshape(8, 16, 128)
        winds, one_step, two_steps = rows_of(uv, j0), rows_of(a1, j0), rows_of(a2p, j0)
        sea, icy = rows_of(m1, j0), rows_of(m2, j0)
        drags, gaps, stresses, heats = [], [], [], []
        for k in range(8):
            rel = winds[k] - block[k, 0:8]
            tile = block[k, 8:16]
            turned = pltpu.roll(tile, 4, 0)
            target = jnp.where(upper, tile, 0.5 * turned)
            ice = jnp.where(upper, turned, tile)
            square = rel * rel
            speed = jnp.sqrt(square + pltpu.roll(square, 4, 0) + 1.0)
            d = coef * speed * (sea[k] - icy[k] * ice)
            drags.append(d)
            stresses.append(2.0 * d * rel)
            gaps.append(target - two_steps[k])
            heats.append(d * (target - one_step[k]))
        put(drag, j0, jnp.stack(drags))
        put(gap, j0, jnp.stack(gaps))
        put(h1, j0, jnp.stack(heats))
        stress[ix, pl.ds(iz, 2)] = jnp.stack(stresses).reshape(2, 4, 8, 128)
        return pack(packed, j0, heats)

    edge[5] = lax.fori_loop(0, LAT // 8, fluxes, zero)
    halos = exchange(5, 1, 2)

    def scatter(k, source):
        return [
            begin(
                remote(
                    source.at[(x + a) % 4, :, (y + b) % 4],
                    got.at[k, n],
                    red_send.at[k, n],
                    red_recv.at[k, n],
                    xy_peer(a, b),
                )
            )
            for n, (a, b) in enumerate(XY)
        ]

    def reduce(k, source, copies):
        total = source[x, :, y]
        for n, copy in enumerate(copies):
            copy.wait_recv()
            total = total + got[k, n]
        part[k] = total
        return [
            begin(
                remote(
                    part.at[k, (z + d) % 4], got_z.at[k, d - 1], redz_send.at[k, d - 1], redz_recv.at[k, d - 1], z_peer(d)
                )
            )
            for d in (2, 1, 3)
        ]

    def owned(k, copies):
        total = part[k, z]
        for copy, d in zip(copies, (2, 1, 3)):
            copy.wait_recv()
            total = total + got_z[k, d - 1]
        return total * (1.0 / (MEMBERS * STEPS))

    stress_copies = scatter(0, stress)
    close(h1)
    for copy in halos:
        copy.wait_recv()
    halo_h = merge(5)

    def last_step(i, carry):
        j0 = i * 8
        ix, iz = i // 2, (i % 2) * 2
        moved = advect(h1, j0, halo_h)
        second = rows_of(drag, j0) * (rows_of(gap, j0) - C00 * moved)
        heat[ix, pl.ds(iz, 2)] = (rows_of(h1, j0) + second).reshape(2, 4, 8, 128)
        put(final, j0, rows_of(a2q, j0) + D00 * moved + C00 * second)
        return carry

    lax.fori_loop(0, LAT // 8, last_step, 0)
    heat_copies = scatter(1, heat)

    def unspread(i, carry):
        r0 = pl.multiple_of(i * 8, 8)
        for f, target in ((0, out_temp), (1, out_humid)):
            for c in range(4):
                target[0, pl.ds(r0, 8), c * 128 : (c + 1) * 128] = final[
                    pl.ds((r0 + 1) * 8 + 4 * f + c, 8, stride=8), :
                ]
        return carry

    lax.fori_loop(0, LAT // 8, unspread, 0)
    stores = [
        pltpu.make_async_copy(out_temp, out_temp_hbm, out_sem.at[0]),
        pltpu.make_async_copy(out_humid, out_humid_hbm, out_sem.at[1]),
    ]
    for copy in stores:
        copy.start()

    stress_z = reduce(0, stress, stress_copies)
    heat_z = reduce(1, heat, heat_copies)
    flux_ref[8:16, :] = owned(0, stress_z)
    warm = owned(1, heat_z)
    flux_ref[0:8, :] = warm
    sst_new_ref[...] = own_sst[...] - 0.5 * warm[0:4, :]
    for copy in stores:
        copy.wait()
    for copy in sends:
        copy.wait_send()


def on_device(
    air_temp, air_humid, wind, exchange_coef, sea_surface_anomaly, sea_ice, current, surface_mask
):
    f32 = jnp.float32
    tall = pltpu.VMEM((ROWS, 128), f32)
    dma = pltpu.SemaphoreType.DMA
    any_space = pl.BlockSpec(memory_space=pl.ANY)
    vmem = pl.BlockSpec(memory_space=pltpu.VMEM)

    out_temp, out_humid, flux, sst_new = pl.pallas_call(
        kernel,
        out_shape=(
            jax.ShapeDtypeStruct((1, LAT, SLAB), f32),
            jax.ShapeDtypeStruct((1, LAT, SLAB), f32),
            jax.ShapeDtypeStruct((16, 128), f32),
            jax.ShapeDtypeStruct((4, 128), f32),
        ),
        in_specs=[any_space] * 3
        + [pl.BlockSpec(memory_space=pltpu.SMEM)]
        + [any_space] * 4,
        out_specs=(any_space, any_space, vmem, vmem),
        scratch_shapes=[
            pltpu.VMEM((1, LEV, LAT, SLAB), jnp.bfloat16),
            pltpu.VMEM((1, LEV, LAT, SLAB), jnp.bfloat16),
            pltpu.VMEM((1, 2, LAT, SLAB), jnp.bfloat16),
            pltpu.VMEM((LAT, SLAB), jnp.int32),
            pltpu.VMEM((8, 128), f32),
            pltpu.VMEM((4, 128), f32),
            pltpu.VMEM((4, 128), f32),
        ]
        + [tall] * 17
        + [
            pltpu.VMEM((4, 4, 4, 16, 128), f32),
            pltpu.VMEM((4, 4, 4, 8, 128), f32),
            pltpu.VMEM((4, 4, 4, 8, 128), f32),
            pltpu.VMEM((2, 15, 4, 8, 128), f32),
            pltpu.VMEM((2, 4, 8, 128), f32),
            pltpu.VMEM((2, 3, 8, 128), f32),
            pltpu.VMEM((6, 8, 128), f32),
            pltpu.VMEM((2, 6, 8, 128), f32),
            pltpu.VMEM((1, LAT, SLAB), f32),
            pltpu.VMEM((1, LAT, SLAB), f32),
            dma((7,)),
            dma((2,)),
            dma((3,)),
            dma((3,)),
            dma((4, 15)),
            dma((4, 15)),
            dma((3, 2)),
            dma((3, 2)),
            dma((2, 15)),
            dma((2, 15)),
            dma((2, 3)),
            dma((2, 3)),
        ],
        compiler_params=pltpu.CompilerParams(
            collective_id=0, has_side_effects=True, vmem_limit_bytes=56 * 2**20
        ),
        cost_estimate=pl.CostEstimate(flops=20_000_000, bytes_accessed=1_200_000, transcendentals=32_768),
    )(
        air_temp,
        air_humid,
        wind,
        exchange_coef,
        sea_surface_anomaly.reshape(4, 128),
        sea_ice.reshape(4, 128),
        current.reshape(8, 128),
        surface_mask,
    )
    return out_temp, out_humid, flux.reshape(4, 1, SLAB), sst_new.reshape(1, SLAB)


def solution(mesh):
    in_specs = (
        P("member", None, None, "lon"),
        P("member", None, None, "lon"),
        P("member", None, None, "lon"),
        P("member"),
        P("member", "lon"),
        P("member", "lon"),
        P(None, "member", "lon"),
        P(None, "lon"),
    )
    out_specs = (
        P("member", None, "lon"),
        P("member", None, "lon"),
        P(None, "member", "lon"),
        P("member", "lon"),
    )
    return jax.shard_map(
        on_device, mesh=mesh, in_specs=in_specs, out_specs=out_specs, check_vma=False
    )
```

time: 1330 us -> 43.3 us (0.03)
  the two profiles are of different devices: /device:TPU:8 before, /device:TPU:2 now
where the time goes in v1:
time: 43.3 us; the launch traced here: 42.6 us
  Pallas kernels  37.7 us (87%)
  local copies, waits for them, and re-layouts  3.56 us (8%)
  between operations  1.3 us (3%)
    pallas_call x1, Pallas kernels, on_device(): pl.pallas_call(kernel, out_shape=(jax.ShapeDtypeStruct((1, LAT, SLAB), f3...  37.7 us
    unnamed x10, local copies, waits for them, and re-layouts  3.56 us

profile of v1, /device:TPU:2, one launch (start us, length us, event | category | flops | bytes accessed | tf_op | source)
XLA Modules:
  0.0 42.6 jit_solution(4248031560857329083)
XLA Ops:
  1.3 37.7 %shard_map.111 = (f32[1,64,512]{2,1,0:T(8,128)}, f32[1,64,512]{2,1,0:T(8,128)}, f32[16,128]{1,0:T(8,128)}, f32[4,128]{1,0:T(4,128)}) custom-call(bf16[1,4,64,512]{3,2,1,0:T(8,128)(2,1)} %temp_hbm.1, bf16[1,4,64,512]{3,2,1,0:T(8,128)(2,1)} %humid_hbm.1, bf16[1,2,64,512]{3,2,1,0:T(8,128)(2,1)} %wind_hbm.1, f32[1]{0:T(128)S(6)} %copy.17.coef_ref, ...), custom_call_target="tpu_custom_call" | custom-call | flops 20000000 | bytes 1200000 | tf_op jit(solution)/shard_map/pallas_call | solution.py:387
  39.0 0.0 copy-start
  39.0 1.6 %copy.18 = f32[1,64,512]{2,1,0:T(8,128)} copy(f32[1,64,512]{2,1,0:T(8,128)} %get-tuple-element.20) | data formatting | bytes 262144
  40.6 0.0 copy-done
  40.6 0.0 copy-start.1
  40.6 0.7 %copy.19 = f32[1,64,512]{2,1,0:T(8,128)} copy(f32[1,64,512]{2,1,0:T(8,128)S(1)} %copy-done) | data formatting | bytes 262144
  41.3 0.0 copy-done.1
  41.3 0.0 copy-start.2
  41.3 0.6 %copy.20 = f32[4,1,512]{2,1,0:T(1,128)} copy(f32[4,1,512]{2,1,0:T(1,128)S(1)} %bitcast.5) | data formatting | bytes 16384
  41.9 0.1 copy-done.2
  42.0 0.6 %copy.21 = f32[1,512]{1,0:T(1,128)} copy(f32[1,512]{1,0:T(1,128)S(1)} %bitcast.9) | data formatting | bytes 4096
Async XLA Ops:
  39.0 1.6 %copy-start = (f32[1,64,512]{2,1,0:T(8,128)S(1)}, f32[1,64,512]{2,1,0:T(8,128)}, u32[]{:S(2)}) copy-start(f32[1,64,512]{2,1,0:T(8,128)} %get-tuple-element.21) | copy-start | bytes 393220
  40.6 0.7 %copy-start.1 = (f32[16,128]{1,0:T(8,128)S(1)}, f32[16,128]{1,0:T(8,128)}, u32[]{:S(2)}) copy-start(f32[16,128]{1,0:T(8,128)} %get-tuple-element.10) | copy-start | bytes 24580
  41.3 0.7 %copy-start.2 = (f32[4,128]{1,0:T(4,128)S(1)}, f32[4,128]{1,0:T(4,128)}, u32[]{:S(2)}) copy-start(f32[4,128]{1,0:T(4,128)} %get-tuple-element.11) | copy-start | bytes 6148

commit v2 on v1

--- a/solution.py
+++ b/solution.py
@@ -23,9 +23,9 @@
 
 
 def kernel(
-    temp_hbm, humid_hbm, wind_hbm, coef_ref, sst_hbm, ice_hbm, cur_hbm, mask_hbm,
+    temp_hbm, humid_hbm, wind_hbm, coef_hbm, sst_hbm, ice_hbm, cur_hbm, mask_hbm,
     out_temp_hbm, out_humid_hbm, flux_ref, sst_new_ref,
-    temp, humid, wind, mask, own_cur, own_sst, own_ice,
+    temp, humid, wind, mask, own_cur, own_sst, own_ice, coef_ref,
     x0, xp, xq, bp, bq, a1, a2p, a2q, h1, drag, gap, final, uv, ce, cn, m1, m2,
     gathered, stress, heat, got, part, got_z, edge, edge_in, out_temp, out_humid,
     in_sem, out_sem, z_send, z_recv, xy_send, xy_recv, lon_send, lon_recv, red_send, red_recv, redz_send, redz_recv,
@@ -54,6 +54,7 @@
                 (temp_hbm, temp),
                 (humid_hbm, humid),
                 (mask_hbm, mask),
+                (coef_hbm, coef_ref),
             ]
         )
     ]
@@ -87,18 +88,19 @@
         for c in range(4):
             ref[pl.ds(start + c, 8, stride=8), :] = value[:, c * 128 : (c + 1) * 128]
 
-    def rows_of(ref, j0, shift=1):
-        return ref[pl.ds(pl.multiple_of((j0 + shift) * 8, 8), 64), :].reshape(8, 8, 128)
+    def rows_of(ref, j0, shift=1, n=8):
+        return ref[pl.ds(pl.multiple_of((j0 + shift) * 8, 8), 8 * n), :].reshape(n, 8, 128)
 
     def put(ref, j0, value):
-        ref[pl.ds(pl.multiple_of((j0 + 1) * 8, 8), 64), :] = value.reshape(64, 128)
+        n = value.shape[0]
+        ref[pl.ds(pl.multiple_of((j0 + 1) * 8, 8), 8 * n), :] = value.reshape(8 * n, 128)
 
     def close(ref):
         ref[0:8, :] = ref[8:16, :]
         ref[ROWS - 8 : ROWS, :] = ref[ROWS - 16 : ROWS - 8, :]
 
     def pack(packed, j0, tiles):
-        for k in range(8):
+        for k in range(len(tiles)):
             packed = jnp.where(slot_of == j0 + k, pltpu.roll(tiles[k], j0 + k, 1), packed)
         return packed
 
@@ -107,11 +109,11 @@
         from_east = pltpu.roll(pltpu.roll(edge_in[1, i], 3, 0), 127, 1)
         return jnp.where(first_run, from_west, from_east)
 
-    def advect(ref, j0, halo):
-        centre, north, south = rows_of(ref, j0), rows_of(ref, j0, 2), rows_of(ref, j0, 0)
-        eastward, northward = rows_of(ce, j0), rows_of(cn, j0)
+    def advect(ref, j0, halo, n=8):
+        centre, north, south = (rows_of(ref, j0, shift, n) for shift in (1, 2, 0))
+        eastward, northward = rows_of(ce, j0, 1, n), rows_of(cn, j0, 1, n)
         result = []
-        for k in range(8):
+        for k in range(n):
             c = centre[k]
             own_halo = pltpu.roll(halo, (128 - (j0 + k)) % 128, 1)
             right = pltpu.roll(c, 1, 1)
@@ -125,6 +127,48 @@
                 + northward[k] * (north[k] - south[k])
             )
         return jnp.stack(result)
+
+    for copy in loads[:3]:
+        copy.wait()
+    gathered[x, z, y, 0:8, :] = own_cur[...]
+    gathered[x, z, y, 8:12, :] = own_sst[...]
+    gathered[x, z, y, 12:16, :] = own_ice[...]
+
+    pl.semaphore_wait(barrier, len(peers))
+
+    sends = []
+
+    def begin(copy):
+        copy.start()
+        sends.append(copy)
+        return copy
+
+    def forward(i, row_z):
+        row = gathered.at[x, row_z, y]
+        return [
+            begin(remote(row, row, xy_send.at[i, n], xy_recv.at[i, n], xy_peer(a, b)))
+            for n, (a, b) in enumerate(XY)
+        ]
+
+    def exchange(first, count, turn):
+        return [
+            begin(
+                remote(
+                    edge.at[pl.ds(first, count)],
+                    edge_in.at[s, pl.ds(first, count)],
+                    lon_send.at[turn, s],
+                    lon_recv.at[turn, s],
+                    lon_peer(d),
+                )
+            )
+            for s, d in ((0, 1), (1, 3))
+        ]
+
+    own_row = gathered.at[x, z, y]
+    along_z = {
+        d: begin(remote(own_row, own_row, z_send.at[d - 1], z_recv.at[d - 1], z_peer(d))) for d in (2, 1, 3)
+    }
+    gathers = [forward(0, z)]
 
     for copy in loads[3:6]:
         copy.wait()
@@ -164,50 +208,9 @@
     for i in range(3):
         edge[i] = packed[i]
 
-    for copy in loads[:3]:
-        copy.wait()
-    gathered[x, z, y, 0:8, :] = own_cur[...]
-    gathered[x, z, y, 8:12, :] = own_sst[...]
-    gathered[x, z, y, 12:16, :] = own_ice[...]
-
-    pl.semaphore_wait(barrier, len(peers))
-
-    sends = []
-
-    def begin(copy):
-        copy.start()
-        sends.append(copy)
-        return copy
-
-    def forward(i, row_z):
-        row = gathered.at[x, row_z, y]
-        return [
-            begin(remote(row, row, xy_send.at[i, n], xy_recv.at[i, n], xy_peer(a, b)))
-            for n, (a, b) in enumerate(XY)
-        ]
-
-    def exchange(first, count, turn):
-        return [
-            begin(
-                remote(
-                    edge.at[pl.ds(first, count)],
-                    edge_in.at[s, pl.ds(first, count)],
-                    lon_send.at[turn, s],
-                    lon_recv.at[turn, s],
-                    lon_peer(d),
-                )
-            )
-            for s, d in ((0, 1), (1, 3))
-        ]
-
-    own_row = gathered.at[x, z, y]
-    along_z = {
-        d: begin(remote(own_row, own_row, z_send.at[d - 1], z_recv.at[d - 1], z_peer(d))) for d in (2, 1, 3)
-    }
     halos = exchange(0, 3, 0)
-    gathers = forward(0, z)
-
     loads[6].wait()
+    loads[7].wait()
 
     def masks(i, carry):
         r0 = pl.multiple_of(i * 8, 8)
@@ -222,6 +225,10 @@
 
     lax.fori_loop(0, LAT // 8, masks, 0)
 
+    for i, d in ((1, 1), (2, 3), (3, 2)):
+        along_z[d].wait_recv()
+        gathers.append(forward(i, (z - d + 4) % 4))
+
     for copy in halos:
         copy.wait_recv()
     halo = [merge(i) for i in range(3)]
@@ -242,10 +249,6 @@
     close(bp)
     close(bq)
 
-    for i, d in ((1, 1), (2, 3), (3, 2)):
-        along_z[d].wait_recv()
-        gathers += forward(i, (z - d + 4) % 4)
-
     for copy in halos:
         copy.wait_recv()
     halo = [merge(3), merge(4)]
@@ -258,97 +261,100 @@
 
     lax.fori_loop(0, LAT // 8, second_step, 0)
 
-    for copy in gathers:
-        copy.wait_recv()
-
     coef = coef_ref[0]
 
-    def fluxes(i, packed):
-        j0 = i * 8
-        ix, iz = i // 2, (i % 2) * 2
-        block = gathered[ix, pl.ds(iz, 2)].reshape(8, 16, 128)
-        winds, one_step, two_steps = rows_of(uv, j0), rows_of(a1, j0), rows_of(a2p, j0)
-        sea, icy = rows_of(m1, j0), rows_of(m2, j0)
-        drags, gaps, stresses, heats = [], [], [], []
-        for k in range(8):
-            rel = winds[k] - block[k, 0:8]
-            tile = block[k, 8:16]
-            turned = pltpu.roll(tile, 4, 0)
-            target = jnp.where(upper, tile, 0.5 * turned)
-            ice = jnp.where(upper, turned, tile)
-            square = rel * rel
-            speed = jnp.sqrt(square + pltpu.roll(square, 4, 0) + 1.0)
-            d = coef * speed * (sea[k] - icy[k] * ice)
-            drags.append(d)
-            stresses.append(2.0 * d * rel)
-            gaps.append(target - two_steps[k])
-            heats.append(d * (target - one_step[k]))
-        put(drag, j0, jnp.stack(drags))
-        put(gap, j0, jnp.stack(gaps))
-        put(h1, j0, jnp.stack(heats))
-        stress[ix, pl.ds(iz, 2)] = jnp.stack(stresses).reshape(2, 4, 8, 128)
-        return pack(packed, j0, heats)
-
-    edge[5] = lax.fori_loop(0, LAT // 8, fluxes, zero)
+    def fluxes(row_z):
+        def step(ix, packed):
+            j0 = ix * 16 + row_z * 4
+            block = gathered[ix, row_z]
+            winds, one_step, two_steps, sea, icy = (rows_of(ref, j0, 1, 4) for ref in (uv, a1, a2p, m1, m2))
+            drags, gaps, stresses, heats = [], [], [], []
+            for k in range(4):
+                rel = winds[k] - block[k, 0:8]
+                tile = block[k, 8:16]
+                turned = pltpu.roll(tile, 4, 0)
+                target = jnp.where(upper, tile, 0.5 * turned)
+                ice = jnp.where(upper, turned, tile)
+                square = rel * rel
+                speed = jnp.sqrt(square + pltpu.roll(square, 4, 0) + 1.0)
+                d = coef * speed * (sea[k] - icy[k] * ice)
+                drags.append(d)
+                stresses.append(2.0 * d * rel)
+                gaps.append(target - two_steps[k])
+                heats.append(d * (target - one_step[k]))
+            put(drag, j0, jnp.stack(drags))
+            put(gap, j0, jnp.stack(gaps))
+            put(h1, j0, jnp.stack(heats))
+            stress[ix, row_z] = jnp.stack(stresses)
+            return pack(packed, j0, heats)
+
+        return step
+
+    packed_h = zero
+    for copies, d in zip(gathers, (0, 1, 3, 2)):
+        for copy in copies:
+            copy.wait_recv()
+        packed_h = lax.fori_loop(0, 4, fluxes((z - d + 4) % 4), packed_h)
+    edge[5] = packed_h
     halos = exchange(5, 1, 2)
 
-    def scatter(k, source):
+    def scatter(k, source, d):
         return [
             begin(
                 remote(
-                    source.at[(x + a) % 4, :, (y + b) % 4],
-                    got.at[k, n],
-                    red_send.at[k, n],
-                    red_recv.at[k, n],
+                    source.at[(x + a) % 4, (z + d) % 4, (y + b) % 4],
+                    got.at[k, d, n],
+                    red_send.at[k, d, n],
+                    red_recv.at[k, d, n],
                     xy_peer(a, b),
                 )
             )
             for n, (a, b) in enumerate(XY)
         ]
 
-    def reduce(k, source, copies):
-        total = source[x, :, y]
+    def reduce(k, source, copies, d):
+        total = source[x, (z + d) % 4, y]
         for n, copy in enumerate(copies):
             copy.wait_recv()
-            total = total + got[k, n]
-        part[k] = total
-        return [
-            begin(
-                remote(
-                    part.at[k, (z + d) % 4], got_z.at[k, d - 1], redz_send.at[k, d - 1], redz_recv.at[k, d - 1], z_peer(d)
-                )
+            total = total + got[k, d, n]
+        part[k, d] = total
+        if d:
+            return begin(
+                remote(part.at[k, d], got_z.at[k, d - 1], redz_send.at[k, d - 1], redz_recv.at[k, d - 1], z_peer(d))
             )
-            for d in (2, 1, 3)
-        ]
 
     def owned(k, copies):
-        total = part[k, z]
+        total = part[k, 0]
         for copy, d in zip(copies, (2, 1, 3)):
             copy.wait_recv()
             total = total + got_z[k, d - 1]
         return total * (1.0 / (MEMBERS * STEPS))
 
-    stress_copies = scatter(0, stress)
+    stress_copies = [scatter(0, stress, d) for d in (2, 1, 3, 0)]
     close(h1)
     for copy in halos:
         copy.wait_recv()
     halo_h = merge(5)
 
-    def last_step(i, carry):
-        j0 = i * 8
-        ix, iz = i // 2, (i % 2) * 2
-        moved = advect(h1, j0, halo_h)
-        second = rows_of(drag, j0) * (rows_of(gap, j0) - C00 * moved)
-        heat[ix, pl.ds(iz, 2)] = (rows_of(h1, j0) + second).reshape(2, 4, 8, 128)
-        put(final, j0, rows_of(a2q, j0) + D00 * moved + C00 * second)
-        return carry
-
-    lax.fori_loop(0, LAT // 8, last_step, 0)
-    heat_copies = scatter(1, heat)
+    def last_step(row_z):
+        def step(ix, carry):
+            j0 = ix * 16 + row_z * 4
+            moved = advect(h1, j0, halo_h, 4)
+            second = rows_of(drag, j0, 1, 4) * (rows_of(gap, j0, 1, 4) - C00 * moved)
+            heat[ix, row_z] = rows_of(h1, j0, 1, 4) + second
+            put(final, j0, rows_of(a2q, j0, 1, 4) + D00 * moved + C00 * second)
+            return carry
+
+        return step
+
+    heat_copies = []
+    for d in (2, 1, 3, 0):
+        lax.fori_loop(0, 4, last_step((z + d) % 4), 0)
+        heat_copies.append(scatter(1, heat, d))
 
     def unspread(i, carry):
         r0 = pl.multiple_of(i * 8, 8)
-        for f, target in ((0, out_temp), (1, out_humid)):
+        for f, target in ((0, out_temp_hbm), (1, out_humid_hbm)):
             for c in range(4):
                 target[0, pl.ds(r0, 8), c * 128 : (c + 1) * 128] = final[
                     pl.ds((r0 + 1) * 8 + 4 * f + c, 8, stride=8), :
@@ -356,23 +362,19 @@
         return carry
 
     lax.fori_loop(0, LAT // 8, unspread, 0)
-    stores = [
-        pltpu.make_async_copy(out_temp, out_temp_hbm, out_sem.at[0]),
-        pltpu.make_async_copy(out_humid, out_humid_hbm, out_sem.at[1]),
-    ]
-    for copy in stores:
-        copy.start()
-
-    stress_z = reduce(0, stress, stress_copies)
-    heat_z = reduce(1, heat, heat_copies)
+    stress_z = [reduce(0, stress, c, d) for c, d in zip(stress_copies, (2, 1, 3, 0))]
+    heat_z = [reduce(1, heat, c, d) for c, d in zip(heat_copies, (2, 1, 3, 0))]
     flux_ref[8:16, :] = owned(0, stress_z)
     warm = owned(1, heat_z)
     flux_ref[0:8, :] = warm
     sst_new_ref[...] = own_sst[...] - 0.5 * warm[0:4, :]
-    for copy in stores:
-        copy.wait()
     for copy in sends:
         copy.wait_send()
+
+
+def hand_over(*refs):
+    for source, target in zip(refs[:4], refs[4:]):
+        target[...] = source[...]
 
 
 def on_device(
@@ -384,18 +386,17 @@
     any_space = pl.BlockSpec(memory_space=pl.ANY)
     vmem = pl.BlockSpec(memory_space=pltpu.VMEM)
 
-    out_temp, out_humid, flux, sst_new = pl.pallas_call(
+    out_shape = (
+        jax.ShapeDtypeStruct((1, LAT, SLAB), f32),
+        jax.ShapeDtypeStruct((1, LAT, SLAB), f32),
+        jax.ShapeDtypeStruct((16, 128), f32),
+        jax.ShapeDtypeStruct((4, 128), f32),
+    )
+    results = pl.pallas_call(
         kernel,
-        out_shape=(
-            jax.ShapeDtypeStruct((1, LAT, SLAB), f32),
-            jax.ShapeDtypeStruct((1, LAT, SLAB), f32),
-            jax.ShapeDtypeStruct((16, 128), f32),
-            jax.ShapeDtypeStruct((4, 128), f32),
-        ),
-        in_specs=[any_space] * 3
-        + [pl.BlockSpec(memory_space=pltpu.SMEM)]
-        + [any_space] * 4,
-        out_specs=(any_space, any_space, vmem, vmem),
+        out_shape=tuple(pltpu.VMEM(o.shape, o.dtype) for o in out_shape),
+        in_specs=[any_space] * 3 + [pl.BlockSpec(memory_space=pltpu.HBM)] + [any_space] * 4,
+        out_specs=(vmem, vmem, vmem, vmem),
         scratch_shapes=[
             pltpu.VMEM((1, LEV, LAT, SLAB), jnp.bfloat16),
             pltpu.VMEM((1, LEV, LAT, SLAB), jnp.bfloat16),
@@ -404,20 +405,21 @@
             pltpu.VMEM((8, 128), f32),
             pltpu.VMEM((4, 128), f32),
             pltpu.VMEM((4, 128), f32),
+            pltpu.SMEM((1,), f32),
         ]
         + [tall] * 17
         + [
             pltpu.VMEM((4, 4, 4, 16, 128), f32),
             pltpu.VMEM((4, 4, 4, 8, 128), f32),
             pltpu.VMEM((4, 4, 4, 8, 128), f32),
-            pltpu.VMEM((2, 15, 4, 8, 128), f32),
+            pltpu.VMEM((2, 4, 15, 8, 128), f32),
             pltpu.VMEM((2, 4, 8, 128), f32),
             pltpu.VMEM((2, 3, 8, 128), f32),
             pltpu.VMEM((6, 8, 128), f32),
             pltpu.VMEM((2, 6, 8, 128), f32),
             pltpu.VMEM((1, LAT, SLAB), f32),
             pltpu.VMEM((1, LAT, SLAB), f32),
-            dma((7,)),
+            dma((8,)),
             dma((2,)),
             dma((3,)),
             dma((3,)),
@@ -425,8 +427,8 @@
             dma((4, 15)),
             dma((3, 2)),
             dma((3, 2)),
-            dma((2, 15)),
-            dma((2, 15)),
+            dma((2, 4, 15)),
+            dma((2, 4, 15)),
             dma((2, 3)),
             dma((2, 3)),
         ],
@@ -444,6 +446,12 @@
         current.reshape(8, 128),
         surface_mask,
     )
+    out_temp, out_humid, flux, sst_new = pl.pallas_call(
+        hand_over,
+        out_shape=out_shape,
+        in_specs=[vmem] * 4,
+        out_specs=[vmem] * 4,
+    )(*[pltpu.with_memory_space_constraint(r, pltpu.VMEM) for r in results])
     return out_temp, out_humid, flux.reshape(4, 1, SLAB), sst_new.reshape(1, SLAB)
 
 

time: 43.3 us -> 38.6 us (0.89); the launches traced: 42.6 us -> 38.4 us
  local copies, waits for them, and re-layouts: 3.56 us -> 0 us
  Pallas kernels: 37.7 us -> 37.2 us
    unnamed x10 -> x0, local copies, waits for them, and re-layouts: 3.56 us -> none
    pallas_call x1 -> x2, Pallas kernels: 37.7 us -> 37.2 us  [the longest x1 36.4 us: on_device(): pl.pallas_call(kernel, out_shape=tuple((pltpu.VMEM(o.shape, o.dtype) for...]
where the time goes in v2:
time: 38.6 us; the launch traced here: 38.4 us
  Pallas kernels  37.2 us (96%)
  between operations  1.29 us (3%)
    pallas_call x1, Pallas kernels, on_device(): pl.pallas_call(kernel, out_shape=tuple((pltpu.VMEM(o.shape, o.dtype) for...  36.4 us

profile of v2, /device:TPU:2, one launch (start us, length us, event | category | flops | bytes accessed | tf_op | source)
XLA Modules:
  0.0 38.4 jit_solution(10568864558917987502)
XLA Ops:
  1.3 36.4 %shard_map.111 = (f32[1,64,512]{2,1,0:T(8,128)S(1)}, f32[1,64,512]{2,1,0:T(8,128)S(1)}, f32[16,128]{1,0:T(8,128)S(1)}, f32[4,128]{1,0:T(4,128)S(1)}) custom-call(bf16[1,4,64,512]{3,2,1,0:T(8,128)(2,1)} %temp_hbm.1, bf16[1,4,64,512]{3,2,1,0:T(8,128)(2,1)} %humid_hbm.1, bf16[1,2,64,512]{3,2,1,0:T(8,128)(2,1)} %wind_hbm.1, f32[1]{0:T(128)S(6)} %copy.13.coef_hbm, ...), custom_call_target="tpu_custom_call" | custom-call | flops 20000000 | bytes 1200000 | tf_op jit(solution)/shard_map/pallas_call | solution.py:395
  37.7 0.7 %shard_map.112 = (f32[1,64,512]{2,1,0:T(8,128)}, f32[1,64,512]{2,1,0:T(8,128)}, f32[16,128]{1,0:T(8,128)}, f32[4,128]{1,0:T(4,128)}) custom-call(f32[1,64,512]{2,1,0:T(8,128)S(1)} %get-tuple-element.12.refs_0_, f32[1,64,512]{2,1,0:T(8,128)S(1)} %get-tuple-element.13.refs_1_, f32[16,128]{1,0:T(8,128)S(1)} %get-tuple-element.14.refs_2_, ...), custom_call_target="tpu_custom_call" | custom-call | tf_op jit(solution)/shard_map/pallas_call | solution.py:449

commit v3 on v2

--- a/solution.py
+++ b/solution.py
@@ -42,6 +42,15 @@
 
     def lon_peer(d):
         return (m, (lon + d) % 4)
+
+    barrier = pltpu.get_barrier_semaphore()
+    peers = (
+        [z_peer(d) for d in (2, 1, 3)]
+        + [xy_peer(a, b) for a, b in XY]
+        + [lon_peer(d) for d in (1, 3)]
+    )
+    for peer in peers:
+        pl.semaphore_signal(barrier, inc=1, device_id=peer, device_id_type=MESH)
 
     loads = [
         pltpu.make_async_copy(src, dst, in_sem.at[i])
@@ -61,15 +70,6 @@
     for copy in loads:
         copy.start()
 
-    barrier = pltpu.get_barrier_semaphore()
-    peers = (
-        [z_peer(d) for d in (2, 1, 3)]
-        + [xy_peer(a, b) for a, b in XY]
-        + [lon_peer(d) for d in (1, 3)]
-    )
-    for peer in peers:
-        pl.semaphore_signal(barrier, inc=1, device_id=peer, device_id_type=MESH)
-
     def remote(src, dst, send, recv, peer):
         return pltpu.make_async_remote_copy(
             src_ref=src, dst_ref=dst, send_sem=send, recv_sem=recv, device_id=peer, device_id_type=MESH
@@ -82,6 +82,7 @@
     upper = sub < 4
     lane_first = lane == 0
     lane_last = lane == 127
+    second_slot_of = jnp.where(first_run, (lane + 127) % 128, jnp.where(last_run, (lane + 2) % 128, -1))
     slot_of = jnp.where(first_run, lane, jnp.where(last_run, (lane + 1) % 128, -1))
 
     def spread(ref, start, value):
@@ -103,6 +104,23 @@
         for k in range(len(tiles)):
             packed = jnp.where(slot_of == j0 + k, pltpu.roll(tiles[k], j0 + k, 1), packed)
         return packed
+
+    def pack_two(packed, second, j0, tiles):
+        for k in range(len(tiles)):
+            turned = pltpu.roll(tiles[k], j0 + k, 1)
+            packed = jnp.where(slot_of == j0 + k, turned, packed)
+            second = jnp.where(second_slot_of == j0 + k, turned, second)
+        return packed, second
+
+    def align(second):
+        return jnp.where(first_run, pltpu.roll(second, 127, 1), pltpu.roll(second, 1, 1))
+
+    def advect_halo(centre, inner, outer, eastward, northward):
+        west = jnp.where(first_run, outer, inner)
+        east = jnp.where(first_run, inner, outer)
+        north = jnp.where(slot_of == LAT - 1, centre, pltpu.roll(centre, 127, 1))
+        south = jnp.where(slot_of == 0, centre, pltpu.roll(centre, 1, 1))
+        return 0.2 * centre + 0.4 * (west + south) + eastward * (east - west) + northward * (north - south)
 
     def merge(i):
         from_west = pltpu.roll(pltpu.roll(edge_in[0, i], 5, 0), 1, 1)
@@ -201,14 +219,20 @@
 
     def pack_inputs(i, packed):
         j0 = i * 8
-        return tuple(pack(t, j0, rows_of(ref, j0)) for t, ref in zip(packed, (x0, xp, xq)))
+        first, p, p2, q, q2, east, north = packed
+        p, p2 = pack_two(p, p2, j0, rows_of(xp, j0))
+        q, q2 = pack_two(q, q2, j0, rows_of(xq, j0))
+        first, east, north = (
+            pack(t, j0, rows_of(ref, j0)) for t, ref in ((first, x0), (east, ce), (north, cn))
+        )
+        return first, p, p2, q, q2, east, north
 
     zero = jnp.zeros((8, 128), jnp.float32)
-    packed = lax.fori_loop(0, LAT // 8, pack_inputs, (zero, zero, zero))
-    for i in range(3):
-        edge[i] = packed[i]
-
-    halos = exchange(0, 3, 0)
+    packed = lax.fori_loop(0, LAT // 8, pack_inputs, (zero,) * 7)
+    for i in range(7):
+        edge[i] = align(packed[i]) if i in (2, 4) else packed[i]
+
+    halos = exchange(0, 7, 0)
     loads[6].wait()
     loads[7].wait()
 
@@ -231,32 +255,25 @@
 
     for copy in halos:
         copy.wait_recv()
-    halo = [merge(i) for i in range(3)]
-
-    def first_step(i, packed):
+    halo = [merge(i) for i in range(7)]
+    halo_bp = advect_halo(halo[1], edge[1], halo[2], halo[5], halo[6])
+    halo_bq = advect_halo(halo[3], edge[3], halo[4], halo[5], halo[6])
+
+    def first_step(i, carry):
         j0 = i * 8
         put(a1, j0, advect(x0, j0, halo[0]))
-        moved_p = advect(xp, j0, halo[1])
-        put(bp, j0, moved_p)
-        moved_q = advect(xq, j0, halo[2])
-        put(bq, j0, moved_q)
-        return pack(packed[0], j0, moved_p), pack(packed[1], j0, moved_q)
-
-    packed = lax.fori_loop(0, LAT // 8, first_step, (zero, zero))
-    for i in range(2):
-        edge[3 + i] = packed[i]
-    halos = exchange(3, 2, 1)
+        put(bp, j0, advect(xp, j0, halo[1]))
+        put(bq, j0, advect(xq, j0, halo[3]))
+        return carry
+
+    lax.fori_loop(0, LAT // 8, first_step, 0)
     close(bp)
     close(bq)
 
-    for copy in halos:
-        copy.wait_recv()
-    halo = [merge(3), merge(4)]
-
     def second_step(i, carry):
         j0 = i * 8
-        put(a2p, j0, advect(bp, j0, halo[0]))
-        put(a2q, j0, advect(bq, j0, halo[1]))
+        put(a2p, j0, advect(bp, j0, halo_bp))
+        put(a2q, j0, advect(bq, j0, halo_bq))
         return carry
 
     lax.fori_loop(0, LAT // 8, second_step, 0)
@@ -294,9 +311,9 @@
     for copies, d in zip(gathers, (0, 1, 3, 2)):
         for copy in copies:
             copy.wait_recv()
-        packed_h = lax.fori_loop(0, 4, fluxes((z - d + 4) % 4), packed_h)
-    edge[5] = packed_h
-    halos = exchange(5, 1, 2)
+        packed_h = lax.fori_loop(0, 4, fluxes((z - d + 4) % 4), packed_h, unroll=True)
+    edge[7] = packed_h
+    halos = exchange(7, 1, 1)
 
     def scatter(k, source, d):
         return [
@@ -334,7 +351,7 @@
     close(h1)
     for copy in halos:
         copy.wait_recv()
-    halo_h = merge(5)
+    halo_h = merge(7)
 
     def last_step(row_z):
         def step(ix, carry):
@@ -349,7 +366,7 @@
 
     heat_copies = []
     for d in (2, 1, 3, 0):
-        lax.fori_loop(0, 4, last_step((z + d) % 4), 0)
+        lax.fori_loop(0, 4, last_step((z + d) % 4), 0, unroll=True)
         heat_copies.append(scatter(1, heat, d))
 
     def unspread(i, carry):
@@ -363,6 +380,9 @@
 
     lax.fori_loop(0, LAT // 8, unspread, 0)
     stress_z = [reduce(0, stress, c, d) for c, d in zip(stress_copies, (2, 1, 3, 0))]
+    early, sends[:] = sends[:], []
+    for copy in early:
+        copy.wait_send()
     heat_z = [reduce(1, heat, c, d) for c, d in zip(heat_copies, (2, 1, 3, 0))]
     flux_ref[8:16, :] = owned(0, stress_z)
     warm = owned(1, heat_z)
@@ -415,8 +435,8 @@
             pltpu.VMEM((2, 4, 15, 8, 128), f32),
             pltpu.VMEM((2, 4, 8, 128), f32),
             pltpu.VMEM((2, 3, 8, 128), f32),
-            pltpu.VMEM((6, 8, 128), f32),
-            pltpu.VMEM((2, 6, 8, 128), f32),
+            pltpu.VMEM((8, 8, 128), f32),
+            pltpu.VMEM((2, 8, 8, 128), f32),
             pltpu.VMEM((1, LAT, SLAB), f32),
             pltpu.VMEM((1, LAT, SLAB), f32),
             dma((8,)),
@@ -425,8 +445,8 @@
             dma((3,)),
             dma((4, 15)),
             dma((4, 15)),
-            dma((3, 2)),
-            dma((3, 2)),
+            dma((2, 2)),
+            dma((2, 2)),
             dma((2, 4, 15)),
             dma((2, 4, 15)),
             dma((2, 3)),

time: 38.6 us -> 37.4 us (0.969)
  the two profiles are of different devices: /device:TPU:2 before, /device:TPU:1 now
where the time goes in v3:
time: 37.4 us; the launch traced here: 37.3 us
  Pallas kernels  36 us (96%)
  between operations  1.29 us (3%)
    pallas_call x1, Pallas kernels, on_device(): pl.pallas_call(kernel, out_shape=tuple((pltpu.VMEM(o.shape, o.dtype) for...  35.3 us

profile of v3, /device:TPU:1, one launch (start us, length us, event | category | flops | bytes accessed | tf_op | source)
XLA Modules:
  0.0 37.3 jit_solution(7106450786994943245)
XLA Ops:
  1.3 35.3 %shard_map.111 = (f32[1,64,512]{2,1,0:T(8,128)S(1)}, f32[1,64,512]{2,1,0:T(8,128)S(1)}, f32[16,128]{1,0:T(8,128)S(1)}, f32[4,128]{1,0:T(4,128)S(1)}) custom-call(bf16[1,4,64,512]{3,2,1,0:T(8,128)(2,1)} %temp_hbm.1, bf16[1,4,64,512]{3,2,1,0:T(8,128)(2,1)} %humid_hbm.1, bf16[1,2,64,512]{3,2,1,0:T(8,128)(2,1)} %wind_hbm.1, f32[1]{0:T(128)S(6)} %copy.13.coef_hbm, ...), custom_call_target="tpu_custom_call" | custom-call | flops 20000000 | bytes 1200000 | tf_op jit(solution)/shard_map/pallas_call | solution.py:415
  36.5 0.7 %shard_map.112 = (f32[1,64,512]{2,1,0:T(8,128)}, f32[1,64,512]{2,1,0:T(8,128)}, f32[16,128]{1,0:T(8,128)}, f32[4,128]{1,0:T(4,128)}) custom-call(f32[1,64,512]{2,1,0:T(8,128)S(1)} %get-tuple-element.12.refs_0_, f32[1,64,512]{2,1,0:T(8,128)S(1)} %get-tuple-element.13.refs_1_, f32[16,128]{1,0:T(8,128)S(1)} %get-tuple-element.14.refs_2_, ...), custom_call_target="tpu_custom_call" | custom-call | tf_op jit(solution)/shard_map/pallas_call | solution.py:469

commit v4 on v3

--- a/solution.py
+++ b/solution.py
@@ -27,8 +27,8 @@
     out_temp_hbm, out_humid_hbm, flux_ref, sst_new_ref,
     temp, humid, wind, mask, own_cur, own_sst, own_ice, coef_ref,
     x0, xp, xq, bp, bq, a1, a2p, a2q, h1, drag, gap, final, uv, ce, cn, m1, m2,
-    gathered, stress, heat, got, part, got_z, edge, edge_in, out_temp, out_humid,
-    in_sem, out_sem, z_send, z_recv, xy_send, xy_recv, lon_send, lon_recv, red_send, red_recv, redz_send, redz_recv,
+    gathered, stress, heat, got, part, got_z, edge, edge_in, rim, rim_in, rim_z, rim_xy, out_temp, out_humid,
+    in_sem, out_sem, z_send, z_recv, xy_send, xy_recv, lon_send, lon_recv, rim_send, rim_recv, rimxy_send, rimxy_recv, red_send, red_recv, redz_send, redz_recv,
 ):
     m = lax.axis_index("member")
     lon = lax.axis_index("lon")
@@ -43,11 +43,14 @@
     def lon_peer(d):
         return (m, (lon + d) % 4)
 
+    def rim_peer(d, s):
+        return (x * 16 + ((z + d) % 4) * 4 + y, (lon + s) % 4)
+
     barrier = pltpu.get_barrier_semaphore()
     peers = (
         [z_peer(d) for d in (2, 1, 3)]
         + [xy_peer(a, b) for a, b in XY]
-        + [lon_peer(d) for d in (1, 3)]
+        + [rim_peer(d, s) for d in (2, 1, 3, 0) for s in (1, 3)]
     )
     for peer in peers:
         pl.semaphore_signal(barrier, inc=1, device_id=peer, device_id_type=MESH)
@@ -122,10 +125,13 @@
         south = jnp.where(slot_of == 0, centre, pltpu.roll(centre, 1, 1))
         return 0.2 * centre + 0.4 * (west + south) + eastward * (east - west) + northward * (north - south)
 
+    def join(west, east):
+        from_west = pltpu.roll(pltpu.roll(west, 5, 0), 1, 1)
+        from_east = pltpu.roll(pltpu.roll(east, 3, 0), 127, 1)
+        return jnp.where(first_run, from_west, from_east)
+
     def merge(i):
-        from_west = pltpu.roll(pltpu.roll(edge_in[0, i], 5, 0), 1, 1)
-        from_east = pltpu.roll(pltpu.roll(edge_in[1, i], 3, 0), 127, 1)
-        return jnp.where(first_run, from_west, from_east)
+        return join(edge_in[0, i], edge_in[1, i])
 
     def advect(ref, j0, halo, n=8):
         centre, north, south = (rows_of(ref, j0, shift, n) for shift in (1, 2, 0))
@@ -152,6 +158,16 @@
     gathered[x, z, y, 8:12, :] = own_sst[...]
     gathered[x, z, y, 12:16, :] = own_ice[...]
 
+    def own_slots(tile):
+        return jnp.where(slot_of == m, pltpu.roll(tile, m, 1), 0.0)
+
+    rim_tile = own_slots(gathered[x, z, y, 8:16, :])
+    rim[...] = (
+        own_slots(own_cur[...])
+        + pltpu.roll(jnp.where(first_run, rim_tile, 0.0), 1, 0)
+        + pltpu.roll(jnp.where(last_run, rim_tile, 0.0), 7, 0)
+    )
+
     pl.semaphore_wait(barrier, len(peers))
 
     sends = []
@@ -186,6 +202,11 @@
     along_z = {
         d: begin(remote(own_row, own_row, z_send.at[d - 1], z_recv.at[d - 1], z_peer(d))) for d in (2, 1, 3)
     }
+    rims = [
+        begin(remote(rim, rim_in.at[s, d], rim_send.at[s, d], rim_recv.at[s, d], rim_peer(d, shift)))
+        for d in (2, 1, 3, 0)
+        for s, shift in ((0, 1), (1, 3))
+    ]
     gathers = [forward(0, z)]
 
     for copy in loads[3:6]:
@@ -217,22 +238,6 @@
     for ref in (x0, xp, xq):
         close(ref)
 
-    def pack_inputs(i, packed):
-        j0 = i * 8
-        first, p, p2, q, q2, east, north = packed
-        p, p2 = pack_two(p, p2, j0, rows_of(xp, j0))
-        q, q2 = pack_two(q, q2, j0, rows_of(xq, j0))
-        first, east, north = (
-            pack(t, j0, rows_of(ref, j0)) for t, ref in ((first, x0), (east, ce), (north, cn))
-        )
-        return first, p, p2, q, q2, east, north
-
-    zero = jnp.zeros((8, 128), jnp.float32)
-    packed = lax.fori_loop(0, LAT // 8, pack_inputs, (zero,) * 7)
-    for i in range(7):
-        edge[i] = align(packed[i]) if i in (2, 4) else packed[i]
-
-    halos = exchange(0, 7, 0)
     loads[6].wait()
     loads[7].wait()
 
@@ -249,14 +254,41 @@
 
     lax.fori_loop(0, LAT // 8, masks, 0)
 
+    def pack_inputs(i, packed):
+        j0 = i * 8
+        first, first2 = pack_two(packed[0], packed[7], j0, rows_of(x0, j0))
+        p, p2 = pack_two(packed[1], packed[2], j0, rows_of(xp, j0))
+        q, q2 = pack_two(packed[3], packed[4], j0, rows_of(xq, j0))
+        east, north, winds, sea, icy = (
+            pack(packed[t], j0, rows_of(ref, j0)) for t, ref in ((5, ce), (6, cn), (8, uv), (9, m1), (10, m2))
+        )
+        return first, p, p2, q, q2, east, north, first2, winds, sea, icy
+
+    zero = jnp.zeros((8, 128), jnp.float32)
+    packed = lax.fori_loop(0, LAT // 8, pack_inputs, (zero,) * 11)
+    for i in range(11):
+        edge[i] = align(packed[i]) if i in (2, 4, 7) else packed[i]
+
+    halos = exchange(0, 11, 0)
+
     for i, d in ((1, 1), (2, 3), (3, 2)):
         along_z[d].wait_recv()
         gathers.append(forward(i, (z - d + 4) % 4))
 
+    for copy in rims:
+        copy.wait_recv()
+    west_rim, east_rim = (sum(rim_in[s, d] for d in range(4)) for s in range(2))
+    rim_z[...] = jnp.where((sub % 4) >= 2, west_rim, east_rim)
+    rims = [
+        begin(remote(rim_z, rim_xy.at[n], rimxy_send.at[n], rimxy_recv.at[n], xy_peer(a, b)))
+        for n, (a, b) in enumerate(XY)
+    ]
+
     for copy in halos:
         copy.wait_recv()
-    halo = [merge(i) for i in range(7)]
+    halo = [merge(i) for i in range(11)]
     halo_bp = advect_halo(halo[1], edge[1], halo[2], halo[5], halo[6])
+    halo_a1 = advect_halo(halo[0], edge[0], halo[7], halo[5], halo[6])
     halo_bq = advect_halo(halo[3], edge[3], halo[4], halo[5], halo[6])
 
     def first_step(i, carry):
@@ -280,21 +312,23 @@
 
     coef = coef_ref[0]
 
+    def forcing(winds, currents, tile, sea, icy):
+        rel = winds - currents
+        turned = pltpu.roll(tile, 4, 0)
+        target = jnp.where(upper, tile, 0.5 * turned)
+        ice = jnp.where(upper, turned, tile)
+        square = rel * rel
+        speed = jnp.sqrt(square + pltpu.roll(square, 4, 0) + 1.0)
+        return rel, target, coef * speed * (sea - icy * ice)
+
     def fluxes(row_z):
-        def step(ix, packed):
+        def step(ix, carry):
             j0 = ix * 16 + row_z * 4
             block = gathered[ix, row_z]
             winds, one_step, two_steps, sea, icy = (rows_of(ref, j0, 1, 4) for ref in (uv, a1, a2p, m1, m2))
             drags, gaps, stresses, heats = [], [], [], []
             for k in range(4):
-                rel = winds[k] - block[k, 0:8]
-                tile = block[k, 8:16]
-                turned = pltpu.roll(tile, 4, 0)
-                target = jnp.where(upper, tile, 0.5 * turned)
-                ice = jnp.where(upper, turned, tile)
-                square = rel * rel
-                speed = jnp.sqrt(square + pltpu.roll(square, 4, 0) + 1.0)
-                d = coef * speed * (sea[k] - icy[k] * ice)
+                rel, target, d = forcing(winds[k], block[k, 0:8], block[k, 8:16], sea[k], icy[k])
                 drags.append(d)
                 stresses.append(2.0 * d * rel)
                 gaps.append(target - two_steps[k])
@@ -303,17 +337,9 @@
             put(gap, j0, jnp.stack(gaps))
             put(h1, j0, jnp.stack(heats))
             stress[ix, row_z] = jnp.stack(stresses)
-            return pack(packed, j0, heats)
+            return carry
 
         return step
-
-    packed_h = zero
-    for copies, d in zip(gathers, (0, 1, 3, 2)):
-        for copy in copies:
-            copy.wait_recv()
-        packed_h = lax.fori_loop(0, 4, fluxes((z - d + 4) % 4), packed_h, unroll=True)
-    edge[7] = packed_h
-    halos = exchange(7, 1, 1)
 
     def scatter(k, source, d):
         return [
@@ -342,16 +368,26 @@
 
     def owned(k, copies):
         total = part[k, 0]
-        for copy, d in zip(copies, (2, 1, 3)):
-            copy.wait_recv()
+        for d in (1, 3, 2):
+            copies[d].wait_recv()
             total = total + got_z[k, d - 1]
         return total * (1.0 / (MEMBERS * STEPS))
 
-    stress_copies = [scatter(0, stress, d) for d in (2, 1, 3, 0)]
+    stress_copies, heat_copies, stress_z, heat_z = {}, {}, {}, {}
+    for copies, d in zip(gathers, (0, 3, 1, 2)):
+        for copy in copies:
+            copy.wait_recv()
+        lax.fori_loop(0, 4, fluxes((z + d) % 4), 0, unroll=True)
+        stress_copies[d] = scatter(0, stress, d)
     close(h1)
-    for copy in halos:
+
+    far = rim_z[...]
+    for n, copy in enumerate(rims):
         copy.wait_recv()
-    halo_h = merge(7)
+        far = far + rim_xy[n]
+    far_tile = jnp.where(first_run, pltpu.roll(far, 7, 0), pltpu.roll(far, 1, 0))
+    _, target, d_halo = forcing(halo[8], join(far, far), join(far_tile, far_tile), halo[9], halo[10])
+    halo_h = d_halo * (target - halo_a1)
 
     def last_step(row_z):
         def step(ix, carry):
@@ -364,10 +400,9 @@
 
         return step
 
-    heat_copies = []
     for d in (2, 1, 3, 0):
         lax.fori_loop(0, 4, last_step((z + d) % 4), 0, unroll=True)
-        heat_copies.append(scatter(1, heat, d))
+        heat_copies[d] = scatter(1, heat, d)
 
     def unspread(i, carry):
         r0 = pl.multiple_of(i * 8, 8)
@@ -379,11 +414,15 @@
         return carry
 
     lax.fori_loop(0, LAT // 8, unspread, 0)
-    stress_z = [reduce(0, stress, c, d) for c, d in zip(stress_copies, (2, 1, 3, 0))]
+    for d in (0, 3, 1):
+        stress_z[d] = reduce(0, stress, stress_copies[d], d)
     early, sends[:] = sends[:], []
     for copy in early:
         copy.wait_send()
-    heat_z = [reduce(1, heat, c, d) for c, d in zip(heat_copies, (2, 1, 3, 0))]
+    for d in (2, 1, 3, 0):
+        heat_z[d] = reduce(1, heat, heat_copies[d], d)
+        if d == 2:
+            stress_z[d] = reduce(0, stress, stress_copies[d], d)
     flux_ref[8:16, :] = owned(0, stress_z)
     warm = owned(1, heat_z)
     flux_ref[0:8, :] = warm
@@ -435,8 +474,12 @@
             pltpu.VMEM((2, 4, 15, 8, 128), f32),
             pltpu.VMEM((2, 4, 8, 128), f32),
             pltpu.VMEM((2, 3, 8, 128), f32),
-            pltpu.VMEM((8, 8, 128), f32),
-            pltpu.VMEM((2, 8, 8, 128), f32),
+            pltpu.VMEM((11, 8, 128), f32),
+            pltpu.VMEM((2, 11, 8, 128), f32),
+            pltpu.VMEM((8, 128), f32),
+            pltpu.VMEM((2, 4, 8, 128), f32),
+            pltpu.VMEM((8, 128), f32),
+            pltpu.VMEM((15, 8, 128), f32),
             pltpu.VMEM((1, LAT, SLAB), f32),
             pltpu.VMEM((1, LAT, SLAB), f32),
             dma((8,)),
@@ -445,8 +488,12 @@
             dma((3,)),
             dma((4, 15)),
             dma((4, 15)),
-            dma((2, 2)),
-            dma((2, 2)),
+            dma((1, 2)),
+            dma((1, 2)),
+            dma((2, 4)),
+            dma((2, 4)),
+            dma((15,)),
+            dma((15,)),
             dma((2, 4, 15)),
             dma((2, 4, 15)),
             dma((2, 3)),

time: 37.4 us -> 36.5 us (0.976)
  the two profiles are of different devices: /device:TPU:1 before, /device:TPU:2 now
where the time goes in v4:
time: 36.5 us; the launch traced here: 36.4 us
  Pallas kernels  35.1 us (96%)
  between operations  1.29 us (4%)
    pallas_call x1, Pallas kernels, on_device(): pl.pallas_call(kernel, out_shape=tuple((pltpu.VMEM(o.shape, o.dtype) for...  34.4 us

profile of v4, /device:TPU:2, one launch (start us, length us, event | category | flops | bytes accessed | tf_op | source)
XLA Modules:
  0.0 36.4 jit_solution(8459218315689551141)
XLA Ops:
  1.3 34.4 %shard_map.111 = (f32[1,64,512]{2,1,0:T(8,128)S(1)}, f32[1,64,512]{2,1,0:T(8,128)S(1)}, f32[16,128]{1,0:T(8,128)S(1)}, f32[4,128]{1,0:T(4,128)S(1)}) custom-call(bf16[1,4,64,512]{3,2,1,0:T(8,128)(2,1)} %temp_hbm.1, bf16[1,4,64,512]{3,2,1,0:T(8,128)(2,1)} %humid_hbm.1, bf16[1,2,64,512]{3,2,1,0:T(8,128)(2,1)} %wind_hbm.1, f32[1]{0:T(128)S(6)} %copy.13.coef_hbm, ...), custom_call_target="tpu_custom_call" | custom-call | flops 20000000 | bytes 1200000 | tf_op jit(solution)/shard_map/pallas_call | solution.py:454
  35.7 0.7 %shard_map.112 = (f32[1,64,512]{2,1,0:T(8,128)}, f32[1,64,512]{2,1,0:T(8,128)}, f32[16,128]{1,0:T(8,128)}, f32[4,128]{1,0:T(4,128)}) custom-call(f32[1,64,512]{2,1,0:T(8,128)S(1)} %get-tuple-element.12.refs_0_, f32[1,64,512]{2,1,0:T(8,128)S(1)} %get-tuple-element.13.refs_1_, f32[16,128]{1,0:T(8,128)S(1)} %get-tuple-element.14.refs_2_, ...), custom_call_target="tpu_custom_call" | custom-call | tf_op jit(solution)/shard_map/pallas_call | solution.py:516

commit v5 on v4

--- a/solution.py
+++ b/solution.py
@@ -271,7 +271,7 @@
 
     halos = exchange(0, 11, 0)
 
-    for i, d in ((1, 1), (2, 3), (3, 2)):
+    for i, d in ((1, 1), (2, 3)):
         along_z[d].wait_recv()
         gathers.append(forward(i, (z - d + 4) % 4))
 
@@ -283,6 +283,10 @@
         begin(remote(rim_z, rim_xy.at[n], rimxy_send.at[n], rimxy_recv.at[n], xy_peer(a, b)))
         for n, (a, b) in enumerate(XY)
     ]
+
+    along_z[2].wait_recv()
+    gathers.append(forward(3, (z + 2) % 4))
+
 
     for copy in halos:
         copy.wait_recv()
@@ -414,15 +418,13 @@
         return carry
 
     lax.fori_loop(0, LAT // 8, unspread, 0)
-    for d in (0, 3, 1):
+    for d in (0, 3, 1, 2):
         stress_z[d] = reduce(0, stress, stress_copies[d], d)
+    for d in (2, 1, 3, 0):
+        heat_z[d] = reduce(1, heat, heat_copies[d], d)
     early, sends[:] = sends[:], []
     for copy in early:
         copy.wait_send()
-    for d in (2, 1, 3, 0):
-        heat_z[d] = reduce(1, heat, heat_copies[d], d)
-        if d == 2:
-            stress_z[d] = reduce(0, stress, stress_copies[d], d)
     flux_ref[8:16, :] = owned(0, stress_z)
     warm = owned(1, heat_z)
     flux_ref[0:8, :] = warm

time: 36.5 us -> 36.4 us (level)
  no operation moved by 1% of the time
where the time goes in v5:
time: 36.4 us; the launch traced here: 36.3 us
  Pallas kernels  35 us (96%)
  between operations  1.29 us (4%)
    pallas_call x1, Pallas kernels, on_device(): pl.pallas_call(kernel, out_shape=tuple((pltpu.VMEM(o.shape, o.dtype) for...  34.3 us

profile of v5, /device:TPU:2, one launch (start us, length us, event | category | flops | bytes accessed | tf_op | source)
XLA Modules:
  0.0 36.3 jit_solution(16961367925761166733)
XLA Ops:
  1.3 34.3 %shard_map.111 = (f32[1,64,512]{2,1,0:T(8,128)S(1)}, f32[1,64,512]{2,1,0:T(8,128)S(1)}, f32[16,128]{1,0:T(8,128)S(1)}, f32[4,128]{1,0:T(4,128)S(1)}) custom-call(bf16[1,4,64,512]{3,2,1,0:T(8,128)(2,1)} %temp_hbm.1, bf16[1,4,64,512]{3,2,1,0:T(8,128)(2,1)} %humid_hbm.1, bf16[1,2,64,512]{3,2,1,0:T(8,128)(2,1)} %wind_hbm.1, f32[1]{0:T(128)S(6)} %copy.13.coef_hbm, ...), custom_call_target="tpu_custom_call" | custom-call | flops 20000000 | bytes 1200000 | tf_op jit(solution)/shard_map/pallas_call | solution.py:456
  35.5 0.7 %shard_map.112 = (f32[1,64,512]{2,1,0:T(8,128)}, f32[1,64,512]{2,1,0:T(8,128)}, f32[16,128]{1,0:T(8,128)}, f32[4,128]{1,0:T(4,128)}) custom-call(f32[1,64,512]{2,1,0:T(8,128)S(1)} %get-tuple-element.12.refs_0_, f32[1,64,512]{2,1,0:T(8,128)S(1)} %get-tuple-element.13.refs_1_, f32[16,128]{1,0:T(8,128)S(1)} %get-tuple-element.14.refs_2_, ...), custom_call_target="tpu_custom_call" | custom-call | tf_op jit(solution)/shard_map/pallas_call | solution.py:518
